TPU v7x, 32 devices: a whole 2x2x4 slice. The times are simulated.
32 devices in a mesh: section: 2 (over core), ctx: 16 (over z, y, x).
Axes of the slice: x: 2, y: 2, z: 4, core: 2. Of those that a mesh axis runs over, the one named last changes fastest.
Arguments:
- queries: bfloat16 [2, 4096, 1024], P('section', 'ctx'), may hold values from -6 to 6
- keys: bfloat16 [2, 4096, 128], P('section', 'ctx'), may hold values from -6 to 6
- values: bfloat16 [2, 4096, 128], P('section', 'ctx'), may hold values from -6 to 6
- attn_out: bfloat16 [2, 4096, 1024], P('section', 'ctx'), may hold values from -3 to 3
- log_sums: float32 [2, 8, 4096], P('section', None, 'ctx'), may hold values from 2 to 6
- grad_held: bfloat16 [2, 4096, 1024], P('section', 'ctx'), may hold values from -6 to 6
- doc_ids: int32 [4096], P('ctx'), may hold values from 0 to 15, never falling along the last dimension, each value on 1 to 512 neighbouring positions
Outputs:
- grad_queries: bfloat16 [2, 4096, 1024], P('section', 'ctx')
- grad_keys: bfloat16 [2, 4096, 128], P('section', 'ctx')
- grad_values: bfloat16 [2, 4096, 128], P('section', 'ctx')
Inputs may be any that keep to these rules, and one draw needn't show every extreme that they name: `doc_ids`: document numbers never fall along the sequence; every document spans at most 512 positions and one spans exactly 512.
All inputs are finite; a program needn't handle non-finite values.
Results may differ from a plain program's by a relative error of at most 0.0049.
Values may be sent and summed in bfloat16 or wider, within the bound.
No kernel may reach another device: no remote copies, remote signals or barrier semaphores. Data moves between devices by JAX's collectives and lax.ppermute only.
A program may use at most 64 MiB of HBM per device.

v0:
```python
import functools

import jax
import jax.numpy as jnp
from jax import lax
from jax.experimental import pallas as pl
from jax.experimental.pallas import tpu as pltpu
from jax.sharding import PartitionSpec as P

HOPS = 2
ORDERS = ((2, 1), (1, 2))
TABLE_ROWS = 16
LAST_ROW = 0
COUNT_ROW = 8
FACT_ROWS = 8
NONE, FEW_KEYS, FEW_QUERIES, ALL = range(4)
BACK_STRIDE = 4
EARLY_HEADS = 4
LOG2_E = 1.4426950408889634
MASKED = -1e30

F32 = jnp.float32
BF16 = jnp.bfloat16


def from_behind(block, axis, distance):
    devices = range(lax.axis_size(axis))
    route = [((i - distance) % len(devices), i) for i in devices]
    return lax.ppermute(block, axis, route)


def full_routes(sections, shards, by, parity):
    route = {}
    for at in range(0, sections, 2):
        there, back = at + parity, at + 1 - parity
        for c in range(shards - by):
            route[there, c] = (there, c + by)
        free = set(range(shards))
        for last in range(shards - by, shards):
            first = last - shards + by
            way = [(there, last)] + [(back, c) for c in range(last, by - 1, -BACK_STRIDE)] + [(back, first), (there, first)]
            free -= {c for section, c in way if section == back}
            route.update(zip(way, way[1:]))
        for lane in range(BACK_STRIDE):
            rest = [c for c in sorted(free) if c % BACK_STRIDE == lane]
            pairs = [(c, c + 1) for c in rest if c + 1 in free] if by > 1 else []
            if by == 1:
                pairs = list(zip(rest[0::2], rest[1::2])) if len(rest) % 2 == 0 else []
                if not pairs:
                    route.update({(back, c): (back, rest[k - len(rest) + 1]) for k, c in enumerate(rest)})
            for c, d in pairs:
                route.update({(back, c): (back, d), (back, d): (back, c)})
    full = sections * shards
    whole = len(route) == full and len(set(route.values())) == full and all(a != b for a, b in route.items())
    return [(a * shards + c, b * shards + d) for (a, c), (b, d) in sorted(route.items())] if whole else None


def routes_behind(sections, shards, hop, parity):
    whole = sections % 2 == 0 and shards >= 4 * BACK_STRIDE
    route = full_routes(sections, shards, hop, parity) if whole else None
    if route is None:
        route = [(s * shards + c, s * shards + c + hop) for s in range(parity, sections, 2) for c in range(shards - hop)]
    return route


def returned(sums, order):
    sections, shards = lax.axis_size("section"), lax.axis_size("ctx")
    hop_of = lambda section: order[section % 2]
    route = {(s, c): (s, c - hop_of(s)) for s in range(sections) for c in range(hop_of(s), shards)}
    idle = [(s, c) for s in range(sections) for c in range(shards - hop_of(s), shards)]
    for s in range(sections):
        for c in range(hop_of(s)):
            route[s, c] = min(idle, key=lambda there: ((there[1] - c) % 2, abs(there[0] - s)))
            idle.remove(route[s, c])
    return lax.ppermute(sums, ("section", "ctx"), [(s * shards + c, t * shards + d) for (s, c), (t, d) in route.items()])


def dot_nt(a, b):
    return lax.dot_general(a, b, (((1,), (1,)), ((), ())), preferred_element_type=F32)


def dot_nn(a, b):
    return lax.dot_general(a, b, (((1,), (0,)), ((), ())), preferred_element_type=F32)


def pack_kernel(keys, values, docs, packed, docs_row, docs_here, sems):
    rows, width = keys.shape[1:]
    copies = [
        pltpu.make_async_copy(docs, docs_here, sems.at[0]),
        pltpu.make_async_copy(keys.at[0], packed.at[0:rows, :], sems.at[1]),
        pltpu.make_async_copy(values.at[0], packed.at[rows : 2 * rows, :], sems.at[2]),
    ]
    for copy in copies:
        copy.start()
    copies[0].wait()
    numbers = docs_here[...]
    last = jnp.max(numbers, axis=1, keepdims=True)
    last_count = jnp.sum((numbers == last).astype(F32), axis=1, keepdims=True)
    row_at = lax.broadcasted_iota(jnp.int32, (TABLE_ROWS, width), 0)
    table = jnp.where(row_at == COUNT_ROW, last_count, last.astype(F32) + 1)
    packed[2 * rows : 2 * rows + TABLE_ROWS, :] = table.astype(BF16)
    docs_row[...] = jnp.broadcast_to(numbers.astype(F32) + 1, docs_row.shape)
    for copy in copies[1:]:
        copy.wait()


def column_of(row, width):
    rows = row.shape[1]
    column = jnp.transpose(jnp.broadcast_to(row, (width, rows)))
    return jnp.concatenate([column] * (rows // width), axis=1)


def block_grads(queries, grads, log_sums, delta_of, block, bias, score_grads, weights_low, sums, first_key, query_rows, chosen=None):
    rows = queries.shape[1]
    width = block.shape[1]
    chosen = range(log_sums.shape[1]) if chosen is None else chosen
    scale = float(width) ** -0.5
    beside = rows // query_rows
    key_rows = slice(first_key, rows)
    side = lambda pieces: pieces[0] if len(pieces) == 1 else jnp.concatenate(pieces, axis=1)
    under = lambda pieces: pieces[0] if len(pieces) == 1 else jnp.concatenate(pieces, axis=0)
    part = lambda ref, head: ref[0, 0:query_rows, head * width : (head + 1) * width]
    columns = lambda head: slice(head * rows, head * rows + query_rows)
    masked = side([bias[key_rows, 0:query_rows]] * beside)
    for head in chosen[::beside]:
        group = range(head, head + beside)
        g = under([part(grads, h) for h in group])
        delta = side([delta_of(h, part(grads, h))[:, 0:query_rows] for h in group])
        lse = side([log_sums[0, h : h + 1, 0:query_rows] for h in group]) * LOG2_E
        scores = dot_nt(block[key_rows, :], under([part(queries, h) for h in group]))
        weights = jnp.exp2(scores * (scale * LOG2_E) - lse + masked)
        weight_grads = dot_nt(block[rows + first_key : 2 * rows, :], g)
        low = (weights * (weight_grads - delta)).astype(BF16)
        weights = weights.astype(BF16)
        for at, h in enumerate(group):
            here = slice(at * query_rows, (at + 1) * query_rows)
            score_grads[key_rows, columns(h)] = low[:, here]
            weights_low[key_rows, columns(h)] = weights[:, here]
    straight = slice(chosen[0] * rows, (chosen[-1] + 1) * rows)
    everything = lambda ref: ref[key_rows, straight] if beside == 1 else side([ref[key_rows, columns(h)] for h in chosen])
    stacked = lambda ref: under([part(ref, h) for h in chosen])
    sums[key_rows, 0:width] = (dot_nn(everything(score_grads), stacked(queries)) * scale).astype(sums.dtype)
    sums[key_rows, width : 2 * width] = dot_nn(everything(weights_low), stacked(grads)).astype(sums.dtype)


def own_bias(docs_row, width, bias):
    rows = bias.shape[0]
    docs = docs_row[0:1, :]
    key_at = lax.broadcasted_iota(jnp.int32, (rows, rows), 0)
    query_at = lax.broadcasted_iota(jnp.int32, (rows, rows), 1)
    bias[...] = jnp.where((column_of(docs, width) == docs) & (key_at <= query_at), 0.0, MASKED)


def own_kernel(chosen, queries, attn_out, grads, log_sums, docs_row, block, score_grads, sums, deltas, block_again, bias, weights_low):
    rows = queries.shape[1]
    heads = log_sums.shape[1]
    width = block.shape[1]
    block_again[...] = block[...]
    docs = docs_row[0:1, :]
    first_count = jnp.sum((docs == docs[:, 0:1]).astype(F32), axis=1, keepdims=True)
    deltas[heads:, :] = jnp.broadcast_to(first_count, (FACT_ROWS, rows))
    own_bias(docs_row, width, bias)
    one = jnp.ones((8, width), BF16)
    for head in range(heads):
        part = slice(head * width, (head + 1) * width)
        product = grads[0, :, part].astype(F32) * attn_out[0, :, part].astype(F32)
        high = product.astype(BF16)
        low = (product - high.astype(F32)).astype(BF16)
        deltas[head : head + 1, :] = (dot_nt(one, high) + dot_nt(one, low))[0:1]
    delta_of = lambda head, g: deltas[head : head + 1, :]
    block_grads(queries, grads, log_sums, delta_of, block, bias, score_grads, weights_low, sums, 0, rows, chosen)


def rest_kernel(chosen, queries, grads, log_sums, docs_row, deltas, block, before, first_grads, score_grads, sums, bias, weights_low):
    own_bias(docs_row, block.shape[1], bias)
    delta_of = lambda head, g: deltas[head : head + 1, :]
    block_grads(queries, grads, log_sums, delta_of, block, bias, score_grads, weights_low, sums, 0, queries.shape[1], chosen)


def hop_kernel(hop, parity, queries, grads, log_sums, docs_row, deltas, block, before, *refs):
    score_grads, sums, bias, weights_low = refs[-4:]

    def reachable():
        rows = queries.shape[1]
        half = rows // 2
        docs = docs_row[0:1, :]
        table = block[2 * rows : 2 * rows + TABLE_ROWS, :].astype(F32)
        same = (table[LAST_ROW : LAST_ROW + 1, 0:1] == docs[:, 0:1]) & (lax.axis_index("ctx") >= hop)
        key_count = jnp.where(same, table[COUNT_ROW : COUNT_ROW + 1, 0:1], 0.0)
        query_count = deltas[log_sums.shape[1] : log_sums.shape[1] + 1, 0:1]
        key_at = lax.broadcasted_iota(jnp.int32, (rows, rows), 0).astype(F32)
        bias[...] = jnp.where((key_at >= rows - key_count) & (docs == docs[:, 0:1]), 0.0, MASKED)
        some = jnp.where(query_count <= half, FEW_QUERIES, ALL)
        mode = jnp.where(key_count == 0, NONE, jnp.where(key_count <= half, FEW_KEYS, some))[0, 0]
        delta_of = lambda head, g: deltas[head : head + 1, :]
        work = functools.partial(block_grads, queries, grads, log_sums, delta_of, block, bias, score_grads, weights_low, sums)

        @pl.when(mode == NONE)
        def _():
            score_grads[...] = jnp.zeros_like(score_grads)
            sums[...] = jnp.zeros_like(sums)

        @pl.when(mode == FEW_KEYS)
        def _():
            score_grads[0:half, :] = jnp.zeros((half, score_grads.shape[1]), BF16)
            sums[0:half, :] = jnp.zeros((half, sums.shape[1]), BF16)
            work(half, rows)

        @pl.when(mode == FEW_QUERIES)
        def _():
            for head in range(score_grads.shape[1] // rows):
                score_grads[:, head * rows + half : (head + 1) * rows] = jnp.zeros((rows, rows - half), BF16)
            work(0, half)

        if hop < HOPS:

            @pl.when(mode == ALL)
            def _():
                work(0, rows)

    pl.when(lax.axis_index("section") % 2 == parity)(reachable)


def pick(candidates, block):
    for parity, candidate in enumerate(candidates):

        @pl.when(lax.axis_index("section") % 2 == parity)
        def _():
            block[...] = candidate[...]


def query_kernel(own, own_grads, first_grads, second_grads, first_even, first_odd, second_even, second_odd, grad_queries, first, second):
    pick((first_even, first_odd), first)
    pick((second_even, second_odd), second)
    rows = own_grads.shape[0]
    heads = own_grads.shape[1] // rows
    width = own.shape[1]
    scale = float(width) ** -0.5
    turned = [jnp.transpose(block[0:rows, :].astype(F32)).astype(BF16) for block in (own, first, second)]
    for head in range(heads):
        columns = slice(head * rows, (head + 1) * rows)
        total = dot_nn(turned[0], own_grads[:, columns]) + dot_nn(turned[1], first_grads[:, columns]) + dot_nn(turned[2], second_grads[:, columns])
        grad_queries[0, :, head * width : (head + 1) * width] = jnp.transpose(total * scale).astype(BF16)


def reached(order, shards):
    hop = jnp.where(lax.axis_index("section") % 2 == 0, *order)
    return lax.axis_index("ctx") + hop < shards


def fold_kernel(shards, own_sums, rest_sums, first_sums, total):
    total[...] = own_sums[...] + rest_sums[...]

    @pl.when(reached(ORDERS[0], shards))
    def _():
        total[...] += first_sums[...].astype(F32)


def add_kernel(shards, folded, second_sums, grad_keys, grad_values, low, sems):
    rows, width = grad_keys.shape[1:]
    there = reached(ORDERS[1], shards).astype(F32)
    copies = []
    for at, target in enumerate((grad_keys, grad_values)):
        half = slice(at * width, (at + 1) * width)
        low[at] = (folded[:, half] + second_sums[:, half].astype(F32) * there).astype(BF16)
        copies.append(pltpu.make_async_copy(low.at[at], target.at[0], sems.at[at]))
        copies[-1].start()
    for copy in copies:
        copy.wait()


def call(kernel, name, outs, args, flops=0, scratch=(), from_hbm=0, kept=(), limit=8, to_hbm=False):
    args = [pltpu.with_memory_space_constraint(a, pltpu.HBM) for a in args[:from_hbm]] + list(args[from_hbm:])
    moved = sum(a.size * a.dtype.itemsize for a in args)
    vmem = lambda count: [pl.BlockSpec(memory_space=pltpu.VMEM)] * count
    return pl.pallas_call(
        kernel,
        out_shape=outs,
        in_specs=[pl.BlockSpec(memory_space=pltpu.HBM)] * from_hbm + vmem(len(args) - from_hbm + len(kept)),
        out_specs=tuple([pl.BlockSpec(memory_space=pltpu.HBM)] * len(outs) if to_hbm else vmem(len(outs))),
        scratch_shapes=list(scratch),
        input_output_aliases={len(args) + i: i for i in range(len(kept))},
        compiler_params=pltpu.CompilerParams(vmem_limit_bytes=limit * 1024 * 1024),
        cost_estimate=pl.CostEstimate(flops=flops, bytes_accessed=moved, transcendentals=0),
        name=name,
    )(*args, *kept)


def per_device(queries, keys, values, attn_out, log_sums, grad_held, doc_ids):
    rows, width = keys.shape[1:]
    heads = log_sums.shape[1]
    shape = jax.ShapeDtypeStruct
    flops = 2 * heads * rows * rows * width
    score_grads = shape((rows, heads * rows), BF16)
    scratch = [pltpu.VMEM((rows, rows), F32), pltpu.VMEM((rows, heads * rows), BF16)]
    sums = lambda dtype: shape((rows, 2 * width), dtype)

    grads = from_behind(grad_held, "section", -1)
    own, docs_row = call(
        pack_kernel,
        "pack",
        (shape((2 * rows + TABLE_ROWS, width), BF16), shape((8, rows), F32)),
        (keys, values, doc_ids.reshape(1, rows)),
        40 * flops,
        [pltpu.VMEM((1, rows), jnp.int32), pltpu.SemaphoreType.DMA((3,))],
        3,
    )
    sections, shards = lax.axis_size("section"), lax.axis_size("ctx")
    behind = lambda block, order: [
        lax.ppermute(block, ("section", "ctx"), routes_behind(sections, shards, hop, parity)) for parity, hop in enumerate(order)
    ]
    first_order, second_order = ORDERS
    first = behind(own, first_order)
    early = range(EARLY_HEADS * heads // 8)
    late = range(len(early), heads)
    own_grads, own_sums, deltas, own_again = call(
        functools.partial(own_kernel, early),
        "own_block",
        (score_grads, sums(F32), shape((heads + FACT_ROWS, rows), F32), shape(own.shape, BF16)),
        (queries, attn_out, grads, log_sums, docs_row, own),
        4 * flops,
        scratch,
    )
    second = behind(own_again, second_order)

    def block_of(name, order, before, candidates):
        kept = ()
        for parity, (hop, block) in enumerate(zip(order, candidates)):
            args = (queries, grads, log_sums, docs_row, deltas, block, before)
            kept = call(functools.partial(hop_kernel, hop, parity), name, (score_grads, sums(BF16)), args, 4 * flops, scratch, 0, kept)
        return kept

    first_grads, first_sums = block_of("first_block", first_order, own_sums, first)
    first_back = returned(first_sums, first_order)
    second_grads, second_sums = block_of("second_block", second_order, first_sums, second)
    second_back = returned(second_sums, second_order)
    own_grads, rest_sums = call(
        functools.partial(rest_kernel, late),
        "own_rest",
        (score_grads, sums(F32)),
        (queries, grads, log_sums, docs_row, deltas, own, second_sums),
        2 * flops,
        scratch,
        0,
        (own_grads,),
    )
    (grad_queries,) = call(
        query_kernel,
        "query_grads",
        (shape(queries.shape, BF16),),
        (own, own_grads, first_grads, second_grads, *first, *second),
        3 * flops,
        [pltpu.VMEM(own.shape, BF16)] * 2,
    )
    (folded,) = call(functools.partial(fold_kernel, shards), "fold", (sums(F32),), (own_sums, rest_sums, first_back))
    grad_keys, grad_values = call(
        functools.partial(add_kernel, shards),
        "add",
        (shape(keys.shape, BF16), shape(values.shape, BF16)),
        (folded, second_back),
        0,
        [pltpu.VMEM((2, rows, width), BF16), pltpu.SemaphoreType.DMA((2,))],
        to_hbm=True,
    )
    return grad_queries, grad_keys, grad_values


def solution(mesh):
    placed = (
        P("section", "ctx", None),
        P("section", "ctx", None),
        P("section", "ctx", None),
        P("section", "ctx", None),
        P("section", None, "ctx"),
        P("section", "ctx", None),
        P("ctx"),
    )
    return jax.shard_map(
        per_device,
        mesh=mesh,
        in_specs=placed,
        out_specs=(P("section", "ctx", None), P("section", "ctx", None), P("section", "ctx", None)),
        check_vma=False,
    )
```

profile of v0, /device:TPU:0, one launch (start us, length us, event | category | flops | bytes accessed | tf_op | source)
XLA Modules:
  0.0 21.0 jit_solution(4354015714380709741)
XLA Ops:
  0.6 0.5 %collective-permute-start = (bf16[1,256,1024]{2,1,0:T(8,128)(2,1)}, bf16[1,256,1024]{2,1,0:T(8,128)(2,1)S(1)}, u32[]{:S(2)}, u32[]{:S(2)}) collective-permute-start(bf16[1,256,1024]{2,1,0:T(8,128)(2,1)} %param.12), channel_id=1, source_target_pairs={{16,0},{0,16},{17,1},{1,17},{18,2},{2,18},{19,3},{3,19},{20,4},{4,... | collective-permute-start | bytes 1572872 | tf_op jit(solution)/shard_map/ppermute | solution.py:29
  1.2 0.0 copy-start
  1.2 0.0 copy-start.1
  1.2 0.0 copy-start.2
  1.2 1.0 %pack.1 = (bf16[528,128]{1,0:T(8,128)(2,1)S(1)}, f32[8,256]{1,0:T(8,128)S(1)}) custom-call(bf16[1,256,128]{2,1,0:T(8,128)(2,1)} %keys.1, bf16[1,256,128]{2,1,0:T(8,128)(2,1)} %values.1, s32[1,256]{1,0:T(1,128)} %bitcast.1), custom_call_target="tpu_custom_call" | custom-call | flops 5368709120 | bytes 132096 | tf_op jit(solution)/shard_map/pack/pallas_call | solution.py:276
  2.2 2.6 %collective-permute-start.3 = (bf16[528,128]{1,0:T(8,128)(2,1)S(1)}, bf16[528,128]{1,0:T(8,128)(2,1)S(1)}, u32[]{:S(2)}, u32[]{:S(2)}) collective-permute-start(bf16[528,128]{1,0:T(8,128)(2,1)S(1)} %get-tuple-element.21.block.own), channel_id=1, source_target_pairs={{0,2},{1,3},{2,4},{3,5},{4,6},{5,7},{6,8},{7,9},{8,10},{9,11},{10,... | collective-permute-start | bytes 405512 | tf_op jit(solution)/shard_map/ppermute | solution.py:310
  4.8 0.0 collective-permute-start.2
  4.8 0.0 collective-permute-done.grads
  4.8 0.0 copy-done
  4.8 0.0 copy-done.1
  4.8 0.0 copy-done.2
  4.8 1.1 %own_block.1 = (bf16[256,2048]{1,0:T(8,128)(2,1)S(1)}, f32[256,256]{1,0:T(8,128)S(1)}, f32[16,256]{1,0:T(8,128)S(1)}, bf16[528,128]{1,0:T(8,128)(2,1)S(1)}) custom-call(bf16[1,256,1024]{2,1,0:T(8,128)(2,1)S(1)} %copy-done, bf16[1,256,1024]{2,1,0:T(8,128)(2,1)S(1)} %copy-done.2, bf16[1,256,1024]{2,1,0:T(8,128)(2,1)S(1)} %collective-permute-done.grads, ...), custom_call_target="tpu_custom_call" | custom-call | flops 536870912 | bytes 1724416 | tf_op jit(solution)/shard_map/own_block/pallas_call | solution.py:276
  5.9 3.1 %collective-permute-start.4 = (bf16[528,128]{1,0:T(8,128)(2,1)S(1)}, bf16[528,128]{1,0:T(8,128)(2,1)S(1)}, u32[]{:S(2)}, u32[]{:S(2)}) collective-permute-start(bf16[528,128]{1,0:T(8,128)(2,1)S(1)} %get-tuple-element.24), channel_id=1, source_target_pairs={{0,1},{1,2},{2,3},{3,4},{4,5},{5,6},{6,7},{7,8},{8,9},{9,10},{10,1... | collective-permute-start | bytes 405512 | tf_op jit(solution)/shard_map/ppermute | solution.py:310
  9.0 0.0 collective-permute-start.1
  9.0 0.0 collective-permute-done.3.block.first_even
  9.0 0.2 first_block.2
  9.2 1.5 %collective-permute-done.2.block.first_odd = bf16[528,128]{1,0:T(8,128)(2,1)S(1)} collective-permute-done((bf16[528,128]{1,0:T(8,128)(2,1)S(1)}, bf16[528,128]{1,0:T(8,128)(2,1)S(1)}, u32[]{:S(2)}, u32[]{:S(2)}) %collective-permute-start.2) | collective-permute-done | bytes 135200 | tf_op jit(solution)/shard_map/ppermute | solution.py:310
  10.7 4.2 %collective-permute-start.5 = (bf16[256,256]{1,0:T(8,128)(2,1)S(1)}, bf16[256,256]{1,0:T(8,128)(2,1)S(1)}, u32[]{:S(2)}, u32[]{:S(2)}) collective-permute-start(bf16[256,256]{1,0:T(8,128)(2,1)S(1)} %get-tuple-element.28.before), channel_id=1, source_target_pairs={{2,0},{3,1},{4,2},{5,3},{6,4},{7,5},{8,6},{9,7},{10,8},{11,9},{12,... | collective-permute-start | bytes 393224 | tf_op jit(solution)/shard_map/ppermute | solution.py:75
  15.0 0.0 collective-permute-done.4.block.second_even
  15.0 0.2 second_block.2
  15.2 0.0 collective-permute-done.1.block.second_odd
  15.2 1.7 %collective-permute-start.6 = (bf16[256,256]{1,0:T(8,128)(2,1)S(1)}, bf16[256,256]{1,0:T(8,128)(2,1)S(1)}, u32[]{:S(2)}, u32[]{:S(2)}) collective-permute-start(bf16[256,256]{1,0:T(8,128)(2,1)S(1)} %get-tuple-element.31.before), channel_id=1, source_target_pairs={{1,0},{2,1},{3,2},{4,3},{5,4},{6,5},{7,6},{8,7},{9,8},{10,9},{11,1... | collective-permute-start | bytes 393224 | tf_op jit(solution)/shard_map/ppermute | solution.py:75
  16.9 0.8 %own_rest.1 = (bf16[256,2048]{1,0:T(8,128)(2,1)S(1)}, f32[256,256]{1,0:T(8,128)S(1)}) custom-call(bf16[1,256,1024]{2,1,0:T(8,128)(2,1)S(1)} %copy-done, bf16[1,256,1024]{2,1,0:T(8,128)(2,1)S(1)} %collective-permute-done.grads, f32[1,8,256]{2,1,0:T(8,128)S(1)} %copy-done.1, f32[8,256]{1,0:T(8,128)S(1)} %get-tuple-element.22.docs_row, ...), custom_call_target="tpu_custom_call", output_to_operand_aliasing={{0}: (7, {})} | custom-call | flops 268435456 | bytes 1347584 | tf_op jit(solution)/shard_map/own_rest/pallas_call | solution.py:276
  17.6 0.0 collective-permute-done.5.first_sums
  17.7 0.1 fold.1.folded
  17.7 1.5 %query_grads.1 = bf16[1,256,1024]{2,1,0:T(8,128)(2,1)} custom-call(bf16[528,128]{1,0:T(8,128)(2,1)S(1)} %get-tuple-element.21.block.own, bf16[256,2048]{1,0:T(8,128)(2,1)S(1)} %get-tuple-element.33.own_grads, bf16[256,2048]{1,0:T(8,128)(2,1)S(1)} %get-tuple-element.34.first_grads, bf16[256,2048]{1,0:T(8,128)(2,1)S(1)} %get-tuple-element.35.second_grads, ...), custom_call_target="tpu_custom_call" | custom-call | flops 402653184 | bytes 3821568 | tf_op jit(solution)/shard_map/query_grads/pallas_call | solution.py:276
  19.3 1.1 %collective-permute-done.6.second_sums = bf16[256,256]{1,0:T(8,128)(2,1)S(1)} collective-permute-done((bf16[256,256]{1,0:T(8,128)(2,1)S(1)}, bf16[256,256]{1,0:T(8,128)(2,1)S(1)}, u32[]{:S(2)}, u32[]{:S(2)}) %collective-permute-start.6) | collective-permute-done | bytes 131104 | tf_op jit(solution)/shard_map/ppermute | solution.py:75
  20.3 0.7 %add.1 = (bf16[1,256,128]{2,1,0:T(8,128)(2,1)}, bf16[1,256,128]{2,1,0:T(8,128)(2,1)}) custom-call(f32[256,256]{1,0:T(8,128)S(1)} %fold.1.folded, bf16[256,256]{1,0:T(8,128)(2,1)S(1)} %collective-permute-done.6.second_sums), custom_call_target="tpu_custom_call" | custom-call | bytes 393216 | tf_op jit(solution)/shard_map/add/pallas_call | solution.py:276
  (2 shorter events, 0.0 us)
Async XLA Ops:
  0.6 4.2 %collective-permute-start = (bf16[1,256,1024]{2,1,0:T(8,128)(2,1)}, bf16[1,256,1024]{2,1,0:T(8,128)(2,1)S(1)}, u32[]{:S(2)}, u32[]{:S(2)}) collective-permute-start(bf16[1,256,1024]{2,1,0:T(8,128)(2,1)} %param.12), channel_id=1, source_target_pairs={{16,0},{0,16},{17,1},{1,17},{18,2},{2,18},{19,3},{3,19},{20,4},{4,... | collective-permute-start | bytes 1572872 | tf_op jit(solution)/shard_map/ppermute | solution.py:29
  1.2 3.7 %copy-start = (bf16[1,256,1024]{2,1,0:T(8,128)(2,1)S(1)}, bf16[1,256,1024]{2,1,0:T(8,128)(2,1)}, u32[]{:S(2)}) copy-start(bf16[1,256,1024]{2,1,0:T(8,128)(2,1)} %queries.11) | copy-start | bytes 1572868
  1.2 3.7 %copy-start.1 = (f32[1,8,256]{2,1,0:T(8,128)S(1)}, f32[1,8,256]{2,1,0:T(8,128)}, u32[]{:S(2)}) copy-start(f32[1,8,256]{2,1,0:T(8,128)} %log_sums.11) | copy-start | bytes 24580
  1.2 3.7 %copy-start.2 = (bf16[1,256,1024]{2,1,0:T(8,128)(2,1)S(1)}, bf16[1,256,1024]{2,1,0:T(8,128)(2,1)}, u32[]{:S(2)}) copy-start(bf16[1,256,1024]{2,1,0:T(8,128)(2,1)} %attn_out.1) | copy-start | bytes 1572868
  2.2 6.8 %collective-permute-start.3 = (bf16[528,128]{1,0:T(8,128)(2,1)S(1)}, bf16[528,128]{1,0:T(8,128)(2,1)S(1)}, u32[]{:S(2)}, u32[]{:S(2)}) collective-permute-start(bf16[528,128]{1,0:T(8,128)(2,1)S(1)} %get-tuple-element.21.block.own), channel_id=1, source_target_pairs={{0,2},{1,3},{2,4},{3,5},{4,6},{5,7},{6,8},{7,9},{8,10},{9,11},{10,... | collective-permute-start | bytes 405512 | tf_op jit(solution)/shard_map/ppermute | solution.py:310
  4.8 5.9 %collective-permute-start.2 = (bf16[528,128]{1,0:T(8,128)(2,1)S(1)}, bf16[528,128]{1,0:T(8,128)(2,1)S(1)}, u32[]{:S(2)}, u32[]{:S(2)}) collective-permute-start(bf16[528,128]{1,0:T(8,128)(2,1)S(1)} %get-tuple-element.21.block.own), channel_id=1, source_target_pairs={{0,16},{1,5},{2,6},{3,0},{4,8},{5,1},{6,2},{7,3},{8,12},{9,13},{10... | collective-permute-start | bytes 405512 | tf_op jit(solution)/shard_map/ppermute | solution.py:310
  5.9 9.1 %collective-permute-start.4 = (bf16[528,128]{1,0:T(8,128)(2,1)S(1)}, bf16[528,128]{1,0:T(8,128)(2,1)S(1)}, u32[]{:S(2)}, u32[]{:S(2)}) collective-permute-start(bf16[528,128]{1,0:T(8,128)(2,1)S(1)} %get-tuple-element.24), channel_id=1, source_target_pairs={{0,1},{1,2},{2,3},{3,4},{4,5},{5,6},{6,7},{7,8},{8,9},{9,10},{10,1... | collective-permute-start | bytes 405512 | tf_op jit(solution)/shard_map/ppermute | solution.py:310
  9.0 6.1 %collective-permute-start.1 = (bf16[528,128]{1,0:T(8,128)(2,1)S(1)}, bf16[528,128]{1,0:T(8,128)(2,1)S(1)}, u32[]{:S(2)}, u32[]{:S(2)}) collective-permute-start(bf16[528,128]{1,0:T(8,128)(2,1)S(1)} %get-tuple-element.24), channel_id=1, source_target_pairs={{0,16},{1,17},{2,0},{3,1},{4,5},{5,4},{6,2},{7,3},{8,9},{9,8},{10,... | collective-permute-start | bytes 405512 | tf_op jit(solution)/shard_map/ppermute | solution.py:310
  10.7 6.9 %collective-permute-start.5 = (bf16[256,256]{1,0:T(8,128)(2,1)S(1)}, bf16[256,256]{1,0:T(8,128)(2,1)S(1)}, u32[]{:S(2)}, u32[]{:S(2)}) collective-permute-start(bf16[256,256]{1,0:T(8,128)(2,1)S(1)} %get-tuple-element.28.before), channel_id=1, source_target_pairs={{2,0},{3,1},{4,2},{5,3},{6,4},{7,5},{8,6},{9,7},{10,8},{11,9},{12,... | collective-permute-start | bytes 393224 | tf_op jit(solution)/shard_map/ppermute | solution.py:75
  15.2 5.1 %collective-permute-start.6 = (bf16[256,256]{1,0:T(8,128)(2,1)S(1)}, bf16[256,256]{1,0:T(8,128)(2,1)S(1)}, u32[]{:S(2)}, u32[]{:S(2)}) collective-permute-start(bf16[256,256]{1,0:T(8,128)(2,1)S(1)} %get-tuple-element.31.before), channel_id=1, source_target_pairs={{1,0},{2,1},{3,2},{4,3},{5,4},{6,5},{7,6},{8,7},{9,8},{10,9},{11,1... | collective-permute-start | bytes 393224 | tf_op jit(solution)/shard_map/ppermute | solution.py:75
where the time goes:
time: 21.3 us; the launch traced here: 21 us
  starting transfers between devices  12.1 us (57%)
  Pallas kernels  5.52 us (26%)
  waiting for transfers between devices  2.66 us (12%)
  between operations  0.71 us (3%)
    ppermute x2, starting transfers between devices, returned(): lax.ppermute(sums, ('section', 'ctx'), [(s * shards + c, t * shards + d)...  5.89 us
    ppermute x4, starting transfers between devices, per_device(): lax.ppermute(block, ('section', 'ctx'), routes_behind(sections, shards, h...  5.72 us
    pallas_call x10, Pallas kernels, call(): pl.pallas_call(kernel, out_shape=outs, in_specs=[pl.BlockSpec(memory_spac...  5.52 us
    ppermute x4, waiting for transfers between devices, per_device(): lax.ppermute(block, ('section', 'ctx'), routes_behind(sections, shards, h...  1.54 us
    ppermute x2, waiting for transfers between devices, returned(): lax.ppermute(sums, ('section', 'ctx'), [(s * shards + c, t * shards + d)...  1.11 us
    ppermute x1, starting transfers between devices, from_behind(): return lax.ppermute(block, axis, route)  0.52 us
  transfers between devices with their start and end apart: 7, of which 2 were waited for; matrix products, arithmetic and copies ran while one was open for 0% of the time, Pallas kernels for 23%

commit v1 on v0

--- a/solution.py
+++ b/solution.py
@@ -70,7 +70,7 @@
     idle = [(s, c) for s in range(sections) for c in range(shards - hop_of(s), shards)]
     for s in range(sections):
         for c in range(hop_of(s)):
-            route[s, c] = min(idle, key=lambda there: ((there[1] - c) % 2, abs(there[0] - s)))
+            route[s, c] = min(idle, key=lambda there: ((there[1] - c) % 2, there))
             idle.remove(route[s, c])
     return lax.ppermute(sums, ("section", "ctx"), [(s * shards + c, t * shards + d) for (s, c), (t, d) in route.items()])
 

time: 21.3 us -> 21.8 us (1.023); the launches traced: 21 us -> 22.1 us
  starting transfers between devices: 12.1 us -> 13 us
  waiting for transfers between devices: 2.66 us -> 2.88 us
    ppermute x2, starting transfers between devices: 5.89 us -> 6.71 us  [returned(): lax.ppermute(sums, ('section', 'ctx'), [(s * shards + c, t * shards + d)...]
    ppermute x2, waiting for transfers between devices: 1.11 us -> 1.33 us  [returned(): lax.ppermute(sums, ('section', 'ctx'), [(s * shards + c, t * shards + d)...]
  transfers between devices with their start and end apart: 7 -> 7, of which waited for: 2 -> 2; matrix products, arithmetic and copies ran while one was open for 0% -> 0% of each run, Pallas kernels for 23% -> 22%
where the time goes in v1:
time: 21.8 us; the launch traced here: 22.1 us
  starting transfers between devices  13 us (60%)
  Pallas kernels  5.52 us (25%)
  waiting for transfers between devices  2.88 us (13%)
  between operations  0.73 us (3%)
    ppermute x2, starting transfers between devices, returned(): lax.ppermute(sums, ('section', 'ctx'), [(s * shards + c, t * shards + d)...  6.71 us
    ppermute x4, starting transfers between devices, per_device(): lax.ppermute(block, ('section', 'ctx'), routes_behind(sections, shards, h...  5.72 us
    pallas_call x10, Pallas kernels, call(): pl.pallas_call(kernel, out_shape=outs, in_specs=[pl.BlockSpec(memory_spac...  5.52 us
    ppermute x4, waiting for transfers between devices, per_device(): lax.ppermute(block, ('section', 'ctx'), routes_behind(sections, shards, h...  1.54 us
    ppermute x2, waiting for transfers between devices, returned(): lax.ppermute(sums, ('section', 'ctx'), [(s * shards + c, t * shards + d)...  1.33 us
    ppermute x1, starting transfers between devices, from_behind(): return lax.ppermute(block, axis, route)  0.52 us
  transfers between devices with their start and end apart: 7, of which 2 were waited for; matrix products, arithmetic and copies ran while one was open for 0% of the time, Pallas kernels for 22%

profile of v1, /device:TPU:0, one launch (start us, length us, event | category | flops | bytes accessed | tf_op | source)
XLA Modules:
  0.0 22.1 jit_solution(14731865484510588906)
XLA Ops:
  0.6 0.5 %collective-permute-start = (bf16[1,256,1024]{2,1,0:T(8,128)(2,1)}, bf16[1,256,1024]{2,1,0:T(8,128)(2,1)S(1)}, u32[]{:S(2)}, u32[]{:S(2)}) collective-permute-start(bf16[1,256,1024]{2,1,0:T(8,128)(2,1)} %param.12), channel_id=1, source_target_pairs={{16,0},{0,16},{17,1},{1,17},{18,2},{2,18},{19,3},{3,19},{20,4},{4,... | collective-permute-start | bytes 1572872 | tf_op jit(solution)/shard_map/ppermute | solution.py:29
  1.2 0.0 copy-start
  1.2 0.0 copy-start.1
  1.2 0.0 copy-start.2
  1.2 1.0 %pack.1 = (bf16[528,128]{1,0:T(8,128)(2,1)S(1)}, f32[8,256]{1,0:T(8,128)S(1)}) custom-call(bf16[1,256,128]{2,1,0:T(8,128)(2,1)} %keys.1, bf16[1,256,128]{2,1,0:T(8,128)(2,1)} %values.1, s32[1,256]{1,0:T(1,128)} %bitcast.1), custom_call_target="tpu_custom_call" | custom-call | flops 5368709120 | bytes 132096 | tf_op jit(solution)/shard_map/pack/pallas_call | solution.py:276
  2.2 2.6 %collective-permute-start.3 = (bf16[528,128]{1,0:T(8,128)(2,1)S(1)}, bf16[528,128]{1,0:T(8,128)(2,1)S(1)}, u32[]{:S(2)}, u32[]{:S(2)}) collective-permute-start(bf16[528,128]{1,0:T(8,128)(2,1)S(1)} %get-tuple-element.21.block.own), channel_id=1, source_target_pairs={{0,2},{1,3},{2,4},{3,5},{4,6},{5,7},{6,8},{7,9},{8,10},{9,11},{10,... | collective-permute-start | bytes 405512 | tf_op jit(solution)/shard_map/ppermute | solution.py:310
  4.8 0.0 collective-permute-start.2
  4.8 0.0 collective-permute-done.grads
  4.8 0.0 copy-done
  4.8 0.0 copy-done.1
  4.8 0.0 copy-done.2
  4.8 1.1 %own_block.1 = (bf16[256,2048]{1,0:T(8,128)(2,1)S(1)}, f32[256,256]{1,0:T(8,128)S(1)}, f32[16,256]{1,0:T(8,128)S(1)}, bf16[528,128]{1,0:T(8,128)(2,1)S(1)}) custom-call(bf16[1,256,1024]{2,1,0:T(8,128)(2,1)S(1)} %copy-done, bf16[1,256,1024]{2,1,0:T(8,128)(2,1)S(1)} %copy-done.2, bf16[1,256,1024]{2,1,0:T(8,128)(2,1)S(1)} %collective-permute-done.grads, ...), custom_call_target="tpu_custom_call" | custom-call | flops 536870912 | bytes 1724416 | tf_op jit(solution)/shard_map/own_block/pallas_call | solution.py:276
  5.9 3.1 %collective-permute-start.4 = (bf16[528,128]{1,0:T(8,128)(2,1)S(1)}, bf16[528,128]{1,0:T(8,128)(2,1)S(1)}, u32[]{:S(2)}, u32[]{:S(2)}) collective-permute-start(bf16[528,128]{1,0:T(8,128)(2,1)S(1)} %get-tuple-element.24), channel_id=1, source_target_pairs={{0,1},{1,2},{2,3},{3,4},{4,5},{5,6},{6,7},{7,8},{8,9},{9,10},{10,1... | collective-permute-start | bytes 405512 | tf_op jit(solution)/shard_map/ppermute | solution.py:310
  9.0 0.0 collective-permute-start.1
  9.0 0.0 collective-permute-done.3.block.first_even
  9.0 0.2 first_block.2
  9.2 1.5 %collective-permute-done.2.block.first_odd = bf16[528,128]{1,0:T(8,128)(2,1)S(1)} collective-permute-done((bf16[528,128]{1,0:T(8,128)(2,1)S(1)}, bf16[528,128]{1,0:T(8,128)(2,1)S(1)}, u32[]{:S(2)}, u32[]{:S(2)}) %collective-permute-start.2) | collective-permute-done | bytes 135200 | tf_op jit(solution)/shard_map/ppermute | solution.py:310
  10.7 5.0 %collective-permute-start.5 = (bf16[256,256]{1,0:T(8,128)(2,1)S(1)}, bf16[256,256]{1,0:T(8,128)(2,1)S(1)}, u32[]{:S(2)}, u32[]{:S(2)}) collective-permute-start(bf16[256,256]{1,0:T(8,128)(2,1)S(1)} %get-tuple-element.28.before), channel_id=1, source_target_pairs={{2,0},{3,1},{4,2},{5,3},{6,4},{7,5},{8,6},{9,7},{10,8},{11,9},{12,... | collective-permute-start | bytes 393224 | tf_op jit(solution)/shard_map/ppermute | solution.py:75
  15.8 0.0 collective-permute-done.4.block.second_even
  15.8 0.2 second_block.2
  16.0 0.0 collective-permute-done.1.block.second_odd
  16.0 1.7 %collective-permute-start.6 = (bf16[256,256]{1,0:T(8,128)(2,1)S(1)}, bf16[256,256]{1,0:T(8,128)(2,1)S(1)}, u32[]{:S(2)}, u32[]{:S(2)}) collective-permute-start(bf16[256,256]{1,0:T(8,128)(2,1)S(1)} %get-tuple-element.31.before), channel_id=1, source_target_pairs={{1,0},{2,1},{3,2},{4,3},{5,4},{6,5},{7,6},{8,7},{9,8},{10,9},{11,1... | collective-permute-start | bytes 393224 | tf_op jit(solution)/shard_map/ppermute | solution.py:75
  17.7 0.8 %own_rest.1 = (bf16[256,2048]{1,0:T(8,128)(2,1)S(1)}, f32[256,256]{1,0:T(8,128)S(1)}) custom-call(bf16[1,256,1024]{2,1,0:T(8,128)(2,1)S(1)} %copy-done, bf16[1,256,1024]{2,1,0:T(8,128)(2,1)S(1)} %collective-permute-done.grads, f32[1,8,256]{2,1,0:T(8,128)S(1)} %copy-done.1, f32[8,256]{1,0:T(8,128)S(1)} %get-tuple-element.22.docs_row, ...), custom_call_target="tpu_custom_call", output_to_operand_aliasing={{0}: (7, {})} | custom-call | flops 268435456 | bytes 1347584 | tf_op jit(solution)/shard_map/own_rest/pallas_call | solution.py:276
  18.5 0.0 collective-permute-done.5.first_sums
  18.5 0.1 fold.1.folded
  18.5 1.5 %query_grads.1 = bf16[1,256,1024]{2,1,0:T(8,128)(2,1)} custom-call(bf16[528,128]{1,0:T(8,128)(2,1)S(1)} %get-tuple-element.21.block.own, bf16[256,2048]{1,0:T(8,128)(2,1)S(1)} %get-tuple-element.33.own_grads, bf16[256,2048]{1,0:T(8,128)(2,1)S(1)} %get-tuple-element.34.first_grads, bf16[256,2048]{1,0:T(8,128)(2,1)S(1)} %get-tuple-element.35.second_grads, ...), custom_call_target="tpu_custom_call" | custom-call | flops 402653184 | bytes 3821568 | tf_op jit(solution)/shard_map/query_grads/pallas_call | solution.py:276
  20.1 1.3 %collective-permute-done.6.second_sums = bf16[256,256]{1,0:T(8,128)(2,1)S(1)} collective-permute-done((bf16[256,256]{1,0:T(8,128)(2,1)S(1)}, bf16[256,256]{1,0:T(8,128)(2,1)S(1)}, u32[]{:S(2)}, u32[]{:S(2)}) %collective-permute-start.6) | collective-permute-done | bytes 131104 | tf_op jit(solution)/shard_map/ppermute | solution.py:75
  21.4 0.7 %add.1 = (bf16[1,256,128]{2,1,0:T(8,128)(2,1)}, bf16[1,256,128]{2,1,0:T(8,128)(2,1)}) custom-call(f32[256,256]{1,0:T(8,128)S(1)} %fold.1.folded, bf16[256,256]{1,0:T(8,128)(2,1)S(1)} %collective-permute-done.6.second_sums), custom_call_target="tpu_custom_call" | custom-call | bytes 393216 | tf_op jit(solution)/shard_map/add/pallas_call | solution.py:276
  (2 shorter events, 0.0 us)
Async XLA Ops:
  0.6 4.2 %collective-permute-start = (bf16[1,256,1024]{2,1,0:T(8,128)(2,1)}, bf16[1,256,1024]{2,1,0:T(8,128)(2,1)S(1)}, u32[]{:S(2)}, u32[]{:S(2)}) collective-permute-start(bf16[1,256,1024]{2,1,0:T(8,128)(2,1)} %param.12), channel_id=1, source_target_pairs={{16,0},{0,16},{17,1},{1,17},{18,2},{2,18},{19,3},{3,19},{20,4},{4,... | collective-permute-start | bytes 1572872 | tf_op jit(solution)/shard_map/ppermute | solution.py:29
  1.2 3.7 %copy-start = (bf16[1,256,1024]{2,1,0:T(8,128)(2,1)S(1)}, bf16[1,256,1024]{2,1,0:T(8,128)(2,1)}, u32[]{:S(2)}) copy-start(bf16[1,256,1024]{2,1,0:T(8,128)(2,1)} %queries.11) | copy-start | bytes 1572868
  1.2 3.7 %copy-start.1 = (f32[1,8,256]{2,1,0:T(8,128)S(1)}, f32[1,8,256]{2,1,0:T(8,128)}, u32[]{:S(2)}) copy-start(f32[1,8,256]{2,1,0:T(8,128)} %log_sums.11) | copy-start | bytes 24580
  1.2 3.7 %copy-start.2 = (bf16[1,256,1024]{2,1,0:T(8,128)(2,1)S(1)}, bf16[1,256,1024]{2,1,0:T(8,128)(2,1)}, u32[]{:S(2)}) copy-start(bf16[1,256,1024]{2,1,0:T(8,128)(2,1)} %attn_out.1) | copy-start | bytes 1572868
  2.2 6.8 %collective-permute-start.3 = (bf16[528,128]{1,0:T(8,128)(2,1)S(1)}, bf16[528,128]{1,0:T(8,128)(2,1)S(1)}, u32[]{:S(2)}, u32[]{:S(2)}) collective-permute-start(bf16[528,128]{1,0:T(8,128)(2,1)S(1)} %get-tuple-element.21.block.own), channel_id=1, source_target_pairs={{0,2},{1,3},{2,4},{3,5},{4,6},{5,7},{6,8},{7,9},{8,10},{9,11},{10,... | collective-permute-start | bytes 405512 | tf_op jit(solution)/shard_map/ppermute | solution.py:310
  4.8 5.9 %collective-permute-start.2 = (bf16[528,128]{1,0:T(8,128)(2,1)S(1)}, bf16[528,128]{1,0:T(8,128)(2,1)S(1)}, u32[]{:S(2)}, u32[]{:S(2)}) collective-permute-start(bf16[528,128]{1,0:T(8,128)(2,1)S(1)} %get-tuple-element.21.block.own), channel_id=1, source_target_pairs={{0,16},{1,5},{2,6},{3,0},{4,8},{5,1},{6,2},{7,3},{8,12},{9,13},{10... | collective-permute-start | bytes 405512 | tf_op jit(solution)/shard_map/ppermute | solution.py:310
  5.9 9.9 %collective-permute-start.4 = (bf16[528,128]{1,0:T(8,128)(2,1)S(1)}, bf16[528,128]{1,0:T(8,128)(2,1)S(1)}, u32[]{:S(2)}, u32[]{:S(2)}) collective-permute-start(bf16[528,128]{1,0:T(8,128)(2,1)S(1)} %get-tuple-element.24), channel_id=1, source_target_pairs={{0,1},{1,2},{2,3},{3,4},{4,5},{5,6},{6,7},{7,8},{8,9},{9,10},{10,1... | collective-permute-start | bytes 405512 | tf_op jit(solution)/shard_map/ppermute | solution.py:310
  9.0 6.9 %collective-permute-start.1 = (bf16[528,128]{1,0:T(8,128)(2,1)S(1)}, bf16[528,128]{1,0:T(8,128)(2,1)S(1)}, u32[]{:S(2)}, u32[]{:S(2)}) collective-permute-start(bf16[528,128]{1,0:T(8,128)(2,1)S(1)} %get-tuple-element.24), channel_id=1, source_target_pairs={{0,16},{1,17},{2,0},{3,1},{4,5},{5,4},{6,2},{7,3},{8,9},{9,8},{10,... | collective-permute-start | bytes 405512 | tf_op jit(solution)/shard_map/ppermute | solution.py:310
  10.7 7.7 %collective-permute-start.5 = (bf16[256,256]{1,0:T(8,128)(2,1)S(1)}, bf16[256,256]{1,0:T(8,128)(2,1)S(1)}, u32[]{:S(2)}, u32[]{:S(2)}) collective-permute-start(bf16[256,256]{1,0:T(8,128)(2,1)S(1)} %get-tuple-element.28.before), channel_id=1, source_target_pairs={{2,0},{3,1},{4,2},{5,3},{6,4},{7,5},{8,6},{9,7},{10,8},{11,9},{12,... | collective-permute-start | bytes 393224 | tf_op jit(solution)/shard_map/ppermute | solution.py:75
  16.0 5.4 %collective-permute-start.6 = (bf16[256,256]{1,0:T(8,128)(2,1)S(1)}, bf16[256,256]{1,0:T(8,128)(2,1)S(1)}, u32[]{:S(2)}, u32[]{:S(2)}) collective-permute-start(bf16[256,256]{1,0:T(8,128)(2,1)S(1)} %get-tuple-element.31.before), channel_id=1, source_target_pairs={{1,0},{2,1},{3,2},{4,3},{5,4},{6,5},{7,6},{8,7},{9,8},{10,9},{11,1... | collective-permute-start | bytes 393224 | tf_op jit(solution)/shard_map/ppermute | solution.py:75

commit v2 on v0

--- a/solution.py
+++ b/solution.py
@@ -321,7 +321,8 @@
         4 * flops,
         scratch,
     )
-    second = behind(own_again, second_order)
+    sent = lambda block, parity: lax.ppermute(block, ("section", "ctx"), routes_behind(sections, shards, second_order[parity], parity))
+    second = [sent(own_again, 0), sent(own, 1)]
 
     def block_of(name, order, before, candidates):
         kept = ()

time: 21.3 us -> 21.9 us (1.028)
  starting transfers between devices: 12.1 us -> 12.9 us
    ppermute x0 -> x2, starting transfers between devices: none -> 3.12 us  [per_device(): lax.ppermute(block, ('section', 'ctx'), routes_behind(sections, shards, s...]
    ppermute x4 -> x2, starting transfers between devices: 5.72 us -> 2.61 us  [per_device(): lax.ppermute(block, ('section', 'ctx'), routes_behind(sections, shards, h...]
    ppermute x2, starting transfers between devices: 5.89 us -> 6.7 us  [returned(): lax.ppermute(sums, ('section', 'ctx'), [(s * shards + c, t * shards + d)...]
    ppermute x4 -> x2, waiting for transfers between devices: 1.54 us -> 1.54 us  [per_device(): lax.ppermute(block, ('section', 'ctx'), routes_behind(sections, shards, h...]
  transfers between devices with their start and end apart: 7 -> 7, of which waited for: 2 -> 3; matrix products, arithmetic and copies ran while one was open for 0% -> 0% of each run, Pallas kernels for 23% -> 22%
where the time goes in v2:
time: 21.9 us; the launch traced here: 21.7 us
  starting transfers between devices  12.9 us (59%)
  Pallas kernels  5.52 us (25%)
  waiting for transfers between devices  2.57 us (12%)
  between operations  0.71 us (3%)
    ppermute x2, starting transfers between devices, returned(): lax.ppermute(sums, ('section', 'ctx'), [(s * shards + c, t * shards + d)...  6.7 us
    pallas_call x10, Pallas kernels, call(): pl.pallas_call(kernel, out_shape=outs, in_specs=[pl.BlockSpec(memory_spac...  5.52 us
    ppermute x2, starting transfers between devices, per_device(): lax.ppermute(block, ('section', 'ctx'), routes_behind(sections, shards, s...  3.12 us
    ppermute x2, starting transfers between devices, per_device(): lax.ppermute(block, ('section', 'ctx'), routes_behind(sections, shards, h...  2.61 us
    ppermute x2, waiting for transfers between devices, per_device(): lax.ppermute(block, ('section', 'ctx'), routes_behind(sections, shards, h...  1.54 us
    ppermute x2, waiting for transfers between devices, returned(): lax.ppermute(sums, ('section', 'ctx'), [(s * shards + c, t * shards + d)...  1.02 us
    ppermute x1, starting transfers between devices, from_behind(): return lax.ppermute(block, axis, route)  0.52 us
  transfers between devices with their start and end apart: 7, of which 3 were waited for; matrix products, arithmetic and copies ran while one was open for 0% of the time, Pallas kernels for 22%

profile of v2, /device:TPU:0, one launch (start us, length us, event | category | flops | bytes accessed | tf_op | source)
XLA Modules:
  0.0 21.7 jit_solution(4539727367915787522)
XLA Ops:
  0.6 0.5 %collective-permute-start = (bf16[1,256,1024]{2,1,0:T(8,128)(2,1)}, bf16[1,256,1024]{2,1,0:T(8,128)(2,1)S(1)}, u32[]{:S(2)}, u32[]{:S(2)}) collective-permute-start(bf16[1,256,1024]{2,1,0:T(8,128)(2,1)} %param.12), channel_id=1, source_target_pairs={{16,0},{0,16},{17,1},{1,17},{18,2},{2,18},{19,3},{3,19},{20,4},{4,... | collective-permute-start | bytes 1572872 | tf_op jit(solution)/shard_map/ppermute | solution.py:29
  1.2 0.0 copy-start
  1.2 0.0 copy-start.1
  1.2 0.0 copy-start.2
  1.2 1.0 %pack.1 = (bf16[528,128]{1,0:T(8,128)(2,1)S(1)}, f32[8,256]{1,0:T(8,128)S(1)}) custom-call(bf16[1,256,128]{2,1,0:T(8,128)(2,1)} %keys.1, bf16[1,256,128]{2,1,0:T(8,128)(2,1)} %values.1, s32[1,256]{1,0:T(1,128)} %bitcast.1), custom_call_target="tpu_custom_call" | custom-call | flops 5368709120 | bytes 132096 | tf_op jit(solution)/shard_map/pack/pallas_call | solution.py:276
  2.2 2.6 %collective-permute-start.3 = (bf16[528,128]{1,0:T(8,128)(2,1)S(1)}, bf16[528,128]{1,0:T(8,128)(2,1)S(1)}, u32[]{:S(2)}, u32[]{:S(2)}) collective-permute-start(bf16[528,128]{1,0:T(8,128)(2,1)S(1)} %get-tuple-element.21.block.own), channel_id=1, source_target_pairs={{0,2},{1,3},{2,4},{3,5},{4,6},{5,7},{6,8},{7,9},{8,10},{9,11},{10,... | collective-permute-start | bytes 405512 | tf_op jit(solution)/shard_map/ppermute | solution.py:310
  4.8 0.0 collective-permute-start.2
  4.8 0.0 collective-permute-done.grads
  4.8 0.0 copy-done
  4.8 0.0 copy-done.1
  4.8 0.0 copy-done.2
  4.8 1.1 %own_block.1 = (bf16[256,2048]{1,0:T(8,128)(2,1)S(1)}, f32[256,256]{1,0:T(8,128)S(1)}, f32[16,256]{1,0:T(8,128)S(1)}, bf16[528,128]{1,0:T(8,128)(2,1)S(1)}) custom-call(bf16[1,256,1024]{2,1,0:T(8,128)(2,1)S(1)} %copy-done, bf16[1,256,1024]{2,1,0:T(8,128)(2,1)S(1)} %copy-done.2, bf16[1,256,1024]{2,1,0:T(8,128)(2,1)S(1)} %collective-permute-done.grads, ...), custom_call_target="tpu_custom_call" | custom-call | flops 536870912 | bytes 1724416 | tf_op jit(solution)/shard_map/own_block/pallas_call | solution.py:276
  5.9 3.1 %collective-permute-start.4 = (bf16[528,128]{1,0:T(8,128)(2,1)S(1)}, bf16[528,128]{1,0:T(8,128)(2,1)S(1)}, u32[]{:S(2)}, u32[]{:S(2)}) collective-permute-start(bf16[528,128]{1,0:T(8,128)(2,1)S(1)} %get-tuple-element.28), channel_id=1, source_target_pairs={{0,1},{1,2},{2,3},{3,4},{4,5},{5,6},{6,7},{7,8},{8,9},{9,10},{10,1... | collective-permute-start | bytes 405512 | tf_op jit(solution)/shard_map/ppermute | solution.py:324
  9.0 0.0 collective-permute-start.1
  9.0 0.0 collective-permute-done.3.block.first_even
  9.0 0.2 first_block.2
  9.2 1.5 %collective-permute-done.2.block.first_odd = bf16[528,128]{1,0:T(8,128)(2,1)S(1)} collective-permute-done((bf16[528,128]{1,0:T(8,128)(2,1)S(1)}, bf16[528,128]{1,0:T(8,128)(2,1)S(1)}, u32[]{:S(2)}, u32[]{:S(2)}) %collective-permute-start.2) | collective-permute-done | bytes 135200 | tf_op jit(solution)/shard_map/ppermute | solution.py:310
  10.7 5.0 %collective-permute-start.5 = (bf16[256,256]{1,0:T(8,128)(2,1)S(1)}, bf16[256,256]{1,0:T(8,128)(2,1)S(1)}, u32[]{:S(2)}, u32[]{:S(2)}) collective-permute-start(bf16[256,256]{1,0:T(8,128)(2,1)S(1)} %get-tuple-element.27.before), channel_id=1, source_target_pairs={{2,0},{3,1},{4,2},{5,3},{6,4},{7,5},{8,6},{9,7},{10,8},{11,9},{12,... | collective-permute-start | bytes 393224 | tf_op jit(solution)/shard_map/ppermute | solution.py:75
  15.8 0.0 collective-permute-done.4.block.second_even
  15.8 0.2 second_block.2
  15.9 0.0 collective-permute-done.1.block.second_odd
  16.0 1.7 %collective-permute-start.6 = (bf16[256,256]{1,0:T(8,128)(2,1)S(1)}, bf16[256,256]{1,0:T(8,128)(2,1)S(1)}, u32[]{:S(2)}, u32[]{:S(2)}) collective-permute-start(bf16[256,256]{1,0:T(8,128)(2,1)S(1)} %get-tuple-element.31.before), channel_id=1, source_target_pairs={{1,0},{2,1},{3,2},{4,3},{5,4},{6,5},{7,6},{8,7},{9,8},{10,9},{11,1... | collective-permute-start | bytes 393224 | tf_op jit(solution)/shard_map/ppermute | solution.py:75
  17.7 0.8 %own_rest.1 = (bf16[256,2048]{1,0:T(8,128)(2,1)S(1)}, f32[256,256]{1,0:T(8,128)S(1)}) custom-call(bf16[1,256,1024]{2,1,0:T(8,128)(2,1)S(1)} %copy-done, bf16[1,256,1024]{2,1,0:T(8,128)(2,1)S(1)} %collective-permute-done.grads, f32[1,8,256]{2,1,0:T(8,128)S(1)} %copy-done.1, f32[8,256]{1,0:T(8,128)S(1)} %get-tuple-element.22.docs_row, ...), custom_call_target="tpu_custom_call", output_to_operand_aliasing={{0}: (7, {})} | custom-call | flops 268435456 | bytes 1347584 | tf_op jit(solution)/shard_map/own_rest/pallas_call | solution.py:276
  18.4 0.8 %collective-permute-done.5.first_sums = bf16[256,256]{1,0:T(8,128)(2,1)S(1)} collective-permute-done((bf16[256,256]{1,0:T(8,128)(2,1)S(1)}, bf16[256,256]{1,0:T(8,128)(2,1)S(1)}, u32[]{:S(2)}, u32[]{:S(2)}) %collective-permute-start.5) | collective-permute-done | bytes 131104 | tf_op jit(solution)/shard_map/ppermute | solution.py:75
  19.2 0.1 fold.1.folded
  19.2 1.5 %query_grads.1 = bf16[1,256,1024]{2,1,0:T(8,128)(2,1)} custom-call(bf16[528,128]{1,0:T(8,128)(2,1)S(1)} %get-tuple-element.21.block.own, bf16[256,2048]{1,0:T(8,128)(2,1)S(1)} %get-tuple-element.33.own_grads, bf16[256,2048]{1,0:T(8,128)(2,1)S(1)} %get-tuple-element.34.first_grads, bf16[256,2048]{1,0:T(8,128)(2,1)S(1)} %get-tuple-element.35.second_grads, ...), custom_call_target="tpu_custom_call" | custom-call | flops 402653184 | bytes 3821568 | tf_op jit(solution)/shard_map/query_grads/pallas_call | solution.py:276
  20.8 0.3 %collective-permute-done.6.second_sums = bf16[256,256]{1,0:T(8,128)(2,1)S(1)} collective-permute-done((bf16[256,256]{1,0:T(8,128)(2,1)S(1)}, bf16[256,256]{1,0:T(8,128)(2,1)S(1)}, u32[]{:S(2)}, u32[]{:S(2)}) %collective-permute-start.6) | collective-permute-done | bytes 131104 | tf_op jit(solution)/shard_map/ppermute | solution.py:75
  21.1 0.7 %add.1 = (bf16[1,256,128]{2,1,0:T(8,128)(2,1)}, bf16[1,256,128]{2,1,0:T(8,128)(2,1)}) custom-call(f32[256,256]{1,0:T(8,128)S(1)} %fold.1.folded, bf16[256,256]{1,0:T(8,128)(2,1)S(1)} %collective-permute-done.6.second_sums), custom_call_target="tpu_custom_call" | custom-call | bytes 393216 | tf_op jit(solution)/shard_map/add/pallas_call | solution.py:276
  (2 shorter events, 0.0 us)
Async XLA Ops:
  0.6 4.2 %collective-permute-start = (bf16[1,256,1024]{2,1,0:T(8,128)(2,1)}, bf16[1,256,1024]{2,1,0:T(8,128)(2,1)S(1)}, u32[]{:S(2)}, u32[]{:S(2)}) collective-permute-start(bf16[1,256,1024]{2,1,0:T(8,128)(2,1)} %param.12), channel_id=1, source_target_pairs={{16,0},{0,16},{17,1},{1,17},{18,2},{2,18},{19,3},{3,19},{20,4},{4,... | collective-permute-start | bytes 1572872 | tf_op jit(solution)/shard_map/ppermute | solution.py:29
  1.2 3.7 %copy-start = (bf16[1,256,1024]{2,1,0:T(8,128)(2,1)S(1)}, bf16[1,256,1024]{2,1,0:T(8,128)(2,1)}, u32[]{:S(2)}) copy-start(bf16[1,256,1024]{2,1,0:T(8,128)(2,1)} %queries.11) | copy-start | bytes 1572868
  1.2 3.7 %copy-start.1 = (f32[1,8,256]{2,1,0:T(8,128)S(1)}, f32[1,8,256]{2,1,0:T(8,128)}, u32[]{:S(2)}) copy-start(f32[1,8,256]{2,1,0:T(8,128)} %log_sums.11) | copy-start | bytes 24580
  1.2 3.7 %copy-start.2 = (bf16[1,256,1024]{2,1,0:T(8,128)(2,1)S(1)}, bf16[1,256,1024]{2,1,0:T(8,128)(2,1)}, u32[]{:S(2)}) copy-start(bf16[1,256,1024]{2,1,0:T(8,128)(2,1)} %attn_out.1) | copy-start | bytes 1572868
  2.2 6.8 %collective-permute-start.3 = (bf16[528,128]{1,0:T(8,128)(2,1)S(1)}, bf16[528,128]{1,0:T(8,128)(2,1)S(1)}, u32[]{:S(2)}, u32[]{:S(2)}) collective-permute-start(bf16[528,128]{1,0:T(8,128)(2,1)S(1)} %get-tuple-element.21.block.own), channel_id=1, source_target_pairs={{0,2},{1,3},{2,4},{3,5},{4,6},{5,7},{6,8},{7,9},{8,10},{9,11},{10,... | collective-permute-start | bytes 405512 | tf_op jit(solution)/shard_map/ppermute | solution.py:310
  4.8 5.9 %collective-permute-start.2 = (bf16[528,128]{1,0:T(8,128)(2,1)S(1)}, bf16[528,128]{1,0:T(8,128)(2,1)S(1)}, u32[]{:S(2)}, u32[]{:S(2)}) collective-permute-start(bf16[528,128]{1,0:T(8,128)(2,1)S(1)} %get-tuple-element.21.block.own), channel_id=1, source_target_pairs={{0,16},{1,5},{2,6},{3,0},{4,8},{5,1},{6,2},{7,3},{8,12},{9,13},{10... | collective-permute-start | bytes 405512 | tf_op jit(solution)/shard_map/ppermute | solution.py:310
  5.9 9.8 %collective-permute-start.4 = (bf16[528,128]{1,0:T(8,128)(2,1)S(1)}, bf16[528,128]{1,0:T(8,128)(2,1)S(1)}, u32[]{:S(2)}, u32[]{:S(2)}) collective-permute-start(bf16[528,128]{1,0:T(8,128)(2,1)S(1)} %get-tuple-element.28), channel_id=1, source_target_pairs={{0,1},{1,2},{2,3},{3,4},{4,5},{5,6},{6,7},{7,8},{8,9},{9,10},{10,1... | collective-permute-start | bytes 405512 | tf_op jit(solution)/shard_map/ppermute | solution.py:324
  9.0 6.9 %collective-permute-start.1 = (bf16[528,128]{1,0:T(8,128)(2,1)S(1)}, bf16[528,128]{1,0:T(8,128)(2,1)S(1)}, u32[]{:S(2)}, u32[]{:S(2)}) collective-permute-start(bf16[528,128]{1,0:T(8,128)(2,1)S(1)} %get-tuple-element.21.block.own), channel_id=1, source_target_pairs={{0,16},{1,17},{2,0},{3,1},{4,5},{5,4},{6,2},{7,3},{8,9},{9,8},{10,... | collective-permute-start | bytes 405512 | tf_op jit(solution)/shard_map/ppermute | solution.py:324
  10.7 8.4 %collective-permute-start.5 = (bf16[256,256]{1,0:T(8,128)(2,1)S(1)}, bf16[256,256]{1,0:T(8,128)(2,1)S(1)}, u32[]{:S(2)}, u32[]{:S(2)}) collective-permute-start(bf16[256,256]{1,0:T(8,128)(2,1)S(1)} %get-tuple-element.27.before), channel_id=1, source_target_pairs={{2,0},{3,1},{4,2},{5,3},{6,4},{7,5},{8,6},{9,7},{10,8},{11,9},{12,... | collective-permute-start | bytes 393224 | tf_op jit(solution)/shard_map/ppermute | solution.py:75
  16.0 5.1 %collective-permute-start.6 = (bf16[256,256]{1,0:T(8,128)(2,1)S(1)}, bf16[256,256]{1,0:T(8,128)(2,1)S(1)}, u32[]{:S(2)}, u32[]{:S(2)}) collective-permute-start(bf16[256,256]{1,0:T(8,128)(2,1)S(1)} %get-tuple-element.31.before), channel_id=1, source_target_pairs={{1,0},{2,1},{3,2},{4,3},{5,4},{6,5},{7,6},{8,7},{9,8},{10,9},{11,1... | collective-permute-start | bytes 393224 | tf_op jit(solution)/shard_map/ppermute | solution.py:75
